TPU v7x, 32 devices: a whole 2x2x4 slice. The times are simulated.
32 devices in a mesh: group: 4 (over y, core), dev: 8 (over z, x).
Axes of the slice: x: 2, y: 2, z: 4, core: 2. Of those that a mesh axis runs over, the one named last changes fastest.
Arguments:
- primary_q: bfloat16 [64, 3584, 1024], P(('group', 'dev')), may hold values from -0.09375 to 0.09375
- primary_scales: bfloat16 [64, 28, 8], P(('group', 'dev')), may hold values from 0.5 to 2
- new_place: int32 [32], P(('group', 'dev')), may hold values from 0 to 63, as said below
- tokens: bfloat16 [512, 3584], P(('group', 'dev')), may hold values from -6 to 6
- experts: int32 [512, 8], P(('group', 'dev')), may hold values from 0 to 63, all different within a row
- replica: int32 [512, 8], P(('group', 'dev')), may hold values from 0 to 1
- route_num: int32 [512, 8], P(('group', 'dev')), may hold values from 1 to 16
Outputs:
- new_weights: bfloat16 [32, 3584, 1024], P(('group', 'dev'))
- new_scales: bfloat16 [32, 28, 8], P(('group', 'dev'))
- hidden_out: bfloat16 [512, 8, 1024], P(('group', 'dev'))
- slot_load: int32 [32, 3], P(('group', 'dev'))
Inputs may be any that keep to these rules, and one draw needn't show every extreme that they name: `new_place`: the redundant slots of the 8 devices of one group hold 8 different experts, each with its primary copy on a device of that group.
All inputs are finite; a program needn't handle non-finite values.
Results may differ from a plain program's by a relative error of at most 0.0057.
Values may be sent and summed in bfloat16 or wider, within the bound.
No kernel may reach another device: no remote copies, remote signals or barrier semaphores. Data moves between devices by JAX's collectives and lax.ppermute only.
A program may use at most 192 MiB of HBM per device.

v0:
```python
import functools

import jax
import jax.numpy as jnp
from jax import lax
from jax.experimental import pallas as pl
from jax.experimental.pallas import tpu as pltpu
from jax.sharding import PartitionSpec as P

TILE = 128
CAP = 2
POOL = 16
VMEM_LIMIT = 60 * 1024 * 1024
AXES = ("group", "dev")
PARTS = (128, 96)


def expert_kernel(x_ref, q_ref, s_ref, o_ref, acc_ref):
    step = pl.program_id(0)

    @pl.when(step == 0)
    def _():
        acc_ref[...] = jnp.zeros_like(acc_ref)

    holding, depth, _ = q_ref.shape
    cells = 2 * CAP
    rows = x_ref.shape[0]
    member_of = lax.broadcasted_iota(jnp.int32, (rows, TILE), 0) // cells % holding
    total = acc_ref[...]
    for member in range(holding):
        for block in range(depth // TILE):
            span = slice(block * TILE, (block + 1) * TILE)
            scale = s_ref[member, 0, block : block + 1, :]
            weights = (q_ref[member, span, :].astype(jnp.float32) * scale).astype(jnp.bfloat16)
            rows_in = jnp.where(member_of == member, x_ref[:, span], jnp.zeros((), jnp.bfloat16))
            total = total + jnp.dot(rows_in, weights, preferred_element_type=jnp.float32)
    acc_ref[...] = total

    @pl.when(step == pl.num_programs(0) - 1)
    def _():
        value = acc_ref[...]
        o_ref[...] = (value / (1.0 + jnp.exp(-value))).astype(jnp.bfloat16)


def serve(rows, values, scales):
    holding, width_in, hidden = values.shape
    depth = 512
    steps = width_in // depth
    count = rows.shape[0]
    wide = jnp.repeat(scales.astype(jnp.float32), TILE, axis=2)
    wide = wide.reshape(holding, steps, depth // TILE, hidden)
    return pl.pallas_call(
        expert_kernel,
        grid=(steps,),
        in_specs=[
            pl.BlockSpec((count, depth), lambda k: (0, k)),
            pl.BlockSpec((holding, depth, hidden), lambda k: (0, k, 0)),
            pl.BlockSpec((holding, 1, depth // TILE, hidden), lambda k: (0, k, 0, 0)),
        ],
        out_specs=pl.BlockSpec((count, hidden), lambda k: (0, 0)),
        out_shape=jax.ShapeDtypeStruct((count, hidden), jnp.bfloat16),
        scratch_shapes=[pltpu.VMEM((count, hidden), jnp.float32)],
        compiler_params=pltpu.CompilerParams(vmem_limit_bytes=VMEM_LIMIT),
        cost_estimate=pl.CostEstimate(
            flops=2 * count * width_in * hidden * holding,
            bytes_accessed=2 * (values.size + count * (width_in + hidden)),
            transcendentals=count * hidden,
        ),
    )(rows, values, wide)


def through_vmem(count, sources, out_at, held, in_sem, out_sem):
    def leave(spot):
        pltpu.make_async_copy(held.at[spot], held.at[spot], in_sem.at[spot]).wait()
        pltpu.make_async_copy(held.at[spot], out_at(spot), out_sem.at[spot]).start()

    def finish(spot):
        pltpu.make_async_copy(held.at[spot], out_at(spot), out_sem.at[spot]).wait()

    for stage in (sources, leave, finish):
        pl.loop(0, count)(stage)


def gather_kernel(index_ref, near_ref, far_ref, out_ref, held, in_sem, out_sem):
    near_count = near_ref.shape[0]

    def start(spot):
        index = index_ref[spot]

        @pl.when(index < near_count)
        def _():
            near_index = jnp.minimum(index, near_count - 1)
            pltpu.make_async_copy(near_ref.at[near_index], held.at[spot], in_sem.at[spot]).start()

        @pl.when(index >= near_count)
        def _():
            far_index = jnp.clip(index - near_count, 0, far_ref.shape[0] - 1)
            pltpu.make_async_copy(far_ref.at[far_index], held.at[spot], in_sem.at[spot]).start()

    through_vmem(out_ref.shape[0], start, lambda spot: out_ref.at[spot], held, in_sem, out_sem)


def gather(indices, near, far):
    count = indices.shape[0]
    anywhere = pl.BlockSpec(memory_space=pl.ANY)
    out = jax.ShapeDtypeStruct((count,) + near.shape[1:], near.dtype)
    return pl.pallas_call(
        gather_kernel,
        in_specs=[pl.BlockSpec(memory_space=pltpu.SMEM), anywhere, anywhere],
        out_specs=anywhere,
        out_shape=out,
        scratch_shapes=[
            pltpu.VMEM(out.shape, out.dtype),
            pltpu.SemaphoreType.DMA((count,)),
            pltpu.SemaphoreType.DMA((count,)),
        ],
        compiler_params=pltpu.CompilerParams(vmem_limit_bytes=VMEM_LIMIT),
        cost_estimate=pl.CostEstimate(
            flops=0, bytes_accessed=4 * out.size, transcendentals=0
        ),
    )(indices, near, far)


def chunk_kernel(first, in_ref, out_ref, held, in_sem, out_sem):
    height = out_ref.shape[2]

    def start(spot):
        pltpu.make_async_copy(
            in_ref.at[:, pl.ds(first + spot * height, height), :], held.at[spot], in_sem.at[spot]
        ).start()

    through_vmem(POOL, start, lambda spot: out_ref.at[spot], held, in_sem, out_sem)


def by_chunk(values, first, height):
    holding, _, hidden = values.shape
    anywhere = pl.BlockSpec(memory_space=pl.ANY)
    out = jax.ShapeDtypeStruct((POOL, holding, height, hidden), values.dtype)
    return pl.pallas_call(
        functools.partial(chunk_kernel, first),
        in_specs=[anywhere],
        out_specs=anywhere,
        out_shape=out,
        scratch_shapes=[
            pltpu.VMEM(out.shape, out.dtype),
            pltpu.SemaphoreType.DMA((POOL,)),
            pltpu.SemaphoreType.DMA((POOL,)),
        ],
        compiler_params=pltpu.CompilerParams(vmem_limit_bytes=VMEM_LIMIT),
        cost_estimate=pl.CostEstimate(
            flops=0, bytes_accessed=4 * out.size, transcendentals=0
        ),
    )(values)


def join_kernel(first, blocks_ref, *refs):
    out_ref, held, in_sem, out_sem = refs[-4:]
    count, height, _ = blocks_ref.shape

    def start(spot):
        pltpu.make_async_copy(blocks_ref.at[spot], held.at[spot], in_sem.at[spot]).start()

    def out_at(spot):
        return out_ref.at[0, pl.ds(first + spot * height, height), :]

    through_vmem(count, start, out_at, held, in_sem, out_sem)


def join(weights, blocks, first, width_in):
    count, _, hidden = blocks.shape
    anywhere = pl.BlockSpec(memory_space=pl.ANY)
    operands = (blocks,) if weights is None else (blocks, weights)
    return pl.pallas_call(
        functools.partial(join_kernel, first),
        in_specs=[anywhere] * len(operands),
        out_specs=anywhere,
        out_shape=jax.ShapeDtypeStruct((1, width_in, hidden), blocks.dtype),
        input_output_aliases={} if weights is None else {1: 0},
        scratch_shapes=[
            pltpu.VMEM(blocks.shape, blocks.dtype),
            pltpu.SemaphoreType.DMA((count,)),
            pltpu.SemaphoreType.DMA((count,)),
        ],
        compiler_params=pltpu.CompilerParams(vmem_limit_bytes=VMEM_LIMIT),
        cost_estimate=pl.CostEstimate(flops=0, bytes_accessed=4 * blocks.size, transcendentals=0),
    )(*operands)


def cross_over(count, leave_rows, give_rows, block, pairs, beside=None, operands=()):
    def branch_of(size):
        def branch(leave_rows, give_rows, block, *operands):
            arrived = block
            if size > 0:
                arrived = lax.ppermute(gather(leave_rows[:size], block, block), AXES, pairs)
            extra = () if beside is None else (beside(*operands),)
            return (gather(give_rows, block, arrived),) + extra

        return branch

    branches = [branch_of(size) for size in range(POOL + 1)]
    return lax.switch(count, branches, leave_rows, give_rows, block, *operands)


def route(experts, replica, place_all, holding):
    pair_count = experts.shape[1]
    device_ids = jnp.arange(place_all.shape[0], dtype=jnp.int32)
    matched = experts[:, :, None] == place_all[None, None, :]
    has_copy = jnp.any(matched, axis=2)
    holder = jnp.sum(jnp.where(matched, device_ids[None, None, :], 0), axis=2)
    use_copy = (replica == 1) & has_copy
    target = jnp.where(use_copy, holder, experts // holding)
    slot_id = jnp.where(use_copy, holding, experts % holding)
    pair_order = jnp.arange(pair_count)
    before = pair_order[:, None] < pair_order[None, :]
    position = jnp.sum((target[:, :, None] == target[:, None, :]) & before[None], axis=1)
    cell = experts % holding * (2 * CAP) + use_copy * CAP + position
    return target, slot_id, position < CAP, cell


def per_device(primary_q, primary_scales, new_place, tokens, experts, replica, route_num):
    holding, width_in, hidden = primary_q.shape
    dev_count = lax.axis_size("dev")
    group_count = lax.axis_size("group")
    device_count = dev_count * group_count
    half = dev_count // 2
    pooled = POOL // half
    my_dev = lax.axis_index("dev")
    my_group = lax.axis_index("group")
    first_dev = my_group * dev_count
    pools = [
        [(base + group) * dev_count + side * half + spot for group in range(pooled) for spot in range(half)]
        for base in range(0, group_count, pooled)
        for side in range(2)
    ]
    over = [
        (group * dev_count + spot, group * dev_count + (spot + half) % dev_count)
        for group in range(group_count)
        for spot in range(dev_count)
    ]

    place_all = lax.all_to_all(
        jnp.broadcast_to(new_place.astype(jnp.bfloat16), (device_count, TILE)),
        AXES,
        split_axis=0,
        concat_axis=0,
        tiled=True,
    )

    spread = []
    start = 0
    for height in PARTS:
        block = by_chunk(primary_q, start, height)
        if not spread:
            block, place_all = lax.optimization_barrier((block, place_all))
        block = lax.all_to_all(
            block, AXES, split_axis=0, concat_axis=0, tiled=True, axis_index_groups=pools
        )
        spread.append(block.reshape(POOL * holding, height, hidden))
        start += POOL * height
    place_all = place_all[:, 0].astype(jnp.int32)
    device_ids = jnp.arange(device_count, dtype=jnp.int32)
    my_id = first_dev + my_dev

    row_count, top_count = experts.shape
    pair_count = row_count * top_count
    scale_cols = primary_scales.size // row_count
    notice = jnp.concatenate(
        [
            experts.astype(jnp.bfloat16),
            replica.astype(jnp.bfloat16),
            primary_scales.reshape(row_count, scale_cols),
        ],
        axis=1,
    )
    notice = jnp.pad(notice, ((0, 0), (0, -notice.shape[1] % TILE)))
    held = jnp.concatenate([tokens, notice], axis=1)
    held = lax.all_gather(held, AXES, axis=0, tiled=True)
    cells = 2 * CAP
    cell_count = device_count * holding * cells

    def pairs_of(held):
        notices = held[:, width_in:].reshape(device_count, row_count, -1)
        experts_all = notices[:, :, :top_count].astype(jnp.int32)
        replica_all = notices[:, :, top_count : 2 * top_count].astype(jnp.int32)
        return [each.reshape(device_count, pair_count) for each in (experts_all, replica_all)]

    def work(held, place_all, values, scales):
        experts_all, replica_all = pairs_of(held)
        _, _, served, cell = route(experts_all, replica_all, place_all, holding)
        mine = served & (experts_all // holding == my_id)
        cell_ids = jnp.arange(holding * cells)
        hit = mine[:, None, :] & (cell[:, None, :] == cell_ids[None, :, None])
        row_at = device_ids[:, None] * row_count + jnp.sum(
            jnp.where(hit, jnp.arange(pair_count) // top_count, 0), axis=2
        )
        row_at = jnp.where(jnp.any(hit, axis=2), row_at, -1).reshape(cell_count)
        row_hits = row_at[:, None] == jnp.arange(device_count * row_count)[None, :]
        rows = jnp.dot(row_hits.astype(jnp.bfloat16), held, preferred_element_type=jnp.float32)
        return serve(rows.astype(jnp.bfloat16), values, scales)

    source = place_all // holding
    dest_side = device_ids % dev_count // half
    source_side = source % dev_count // half
    crossing = source_side != dest_side
    source_row = (source // dev_count % pooled * half + source % half) * holding + place_all % holding
    pool_of = device_ids // dev_count // pooled
    peers = (pool_of[:, None] == pool_of[None, :]) & (dest_side[:, None] == dest_side[None, :])
    ahead = peers & crossing[None, :] & (device_ids[None, :] < device_ids[:, None])
    rank = jnp.sum(ahead, axis=1)
    cross_count = jnp.max(jnp.where(crossing, rank + 1, 0))
    my_side = my_dev // half
    my_pool = my_group // pooled
    leaving = (pool_of == my_pool) & (dest_side != my_side) & crossing
    slots = jnp.arange(POOL)
    leave_rows = jnp.sum(
        jnp.where(leaving[None, :] & (rank[None, :] == slots[:, None]), source_row[None, :], 0), axis=1
    )
    staying = (pool_of == my_pool) & (dest_side == my_side)
    place_in_pool = device_ids // dev_count % pooled * half + device_ids % half
    give_rows = jnp.sum(
        jnp.where(
            staying[None, :] & (place_in_pool[None, :] == slots[:, None]),
            jnp.where(crossing, POOL * holding + rank, source_row)[None, :],
            0,
        ),
        axis=1,
    )
    first, second = spread
    (first,) = cross_over(cross_count, leave_rows, give_rows, first, over)
    first = lax.all_to_all(
        first, AXES, split_axis=0, concat_axis=0, tiled=True, axis_index_groups=pools
    )
    second, activated = cross_over(
        cross_count,
        leave_rows,
        give_rows,
        second,
        over,
        work,
        (held, place_all, primary_q, primary_scales),
    )
    returned = lax.all_to_all(
        activated.reshape(device_count, holding * cells, hidden),
        AXES,
        split_axis=0,
        concat_axis=0,
        tiled=True,
    )
    second, returned, held = lax.optimization_barrier((second, returned, held))
    second = lax.all_to_all(
        second, AXES, split_axis=0, concat_axis=0, tiled=True, axis_index_groups=pools
    )
    new_weights = join(None, first, 0, width_in)
    new_weights = join(new_weights, second, first.shape[0] * first.shape[1], width_in)

    experts_all, replica_all = pairs_of(held)
    target, slot_id, served, _ = route(experts_all, replica_all, place_all, holding)
    arriving = served & (target == my_id)
    slot_load = jnp.stack(
        [jnp.sum((arriving & (slot_id == slot)).astype(jnp.int32)) for slot in range(holding + 1)]
    )[None]
    owner_notice = held[:, width_in:].reshape(device_count, row_count, -1)
    owner_notice = lax.dynamic_index_in_dim(
        owner_notice, new_place[0] // holding, 0, keepdims=False
    )
    owner_scales = owner_notice[:, 2 * top_count : 2 * top_count + scale_cols]
    new_scales = lax.dynamic_index_in_dim(
        owner_scales.reshape(primary_scales.shape), new_place[0] % holding, 0
    )

    my_experts = experts.reshape(1, pair_count)
    _, _, my_served, my_cell = route(
        my_experts, replica.reshape(1, pair_count), place_all, holding
    )
    my_cell = (my_experts // holding * (holding * cells) + my_cell)[0]
    placed = (my_cell[:, None] == jnp.arange(cell_count)[None, :]) & my_served[0][:, None]
    selected = jnp.dot(
        placed.astype(jnp.bfloat16),
        returned.reshape(cell_count, hidden),
        preferred_element_type=jnp.float32,
    )
    weight = route_num.reshape(pair_count).astype(jnp.float32) / 16.0
    hidden_out = (selected * weight[:, None]).astype(jnp.bfloat16)
    hidden_out = hidden_out.reshape(row_count, top_count, hidden)
    return (new_weights, new_scales, hidden_out, slot_load)


def solution(mesh):
    in_specs = (
        P(AXES, None, None),
        P(AXES, None, None),
        P(AXES),
        P(AXES, None),
        P(AXES, None),
        P(AXES, None),
        P(AXES, None),
    )
    out_specs = (
        P(AXES, None, None),
        P(AXES, None, None),
        P(AXES, None, None),
        P(AXES, None),
    )
    return jax.shard_map(
        per_device, mesh=mesh, in_specs=in_specs, out_specs=out_specs, check_vma=False
    )
```

profile of v0, /device:TPU:0, one launch (start us, length us, event | category | flops | bytes accessed | tf_op | source)
XLA Modules:
  0.0 650.9 jit_solution(17673087779972804924)
XLA Ops:
  8.4 7.3 %all-to-all-start = ((bf16[32,1,128]{2,1,0:T(2,128)(2,1)}), bf16[32,1,128]{2,1,0:T(2,128)(2,1)S(1)}, u32[]{:S(2)}, u32[]{:S(2)}) async-start(bf16[32,1,128]{2,1,0:T(2,128)(2,1)} %broadcast_in_dim.632), calls=%async_computation | async-start | bytes 32768 | tf_op jit(solution)/shard_map/all_to_all | solution.py:241
  15.7 5.5 shard_map.103
  21.3 1.5 all-to-all-done
  22.8 4.6 all-to-all-start.1
  27.4 6.5 %shard_map.102 = bf16[16,2,128,1024]{3,2,1,0:T(8,128)(2,1)} custom-call(bf16[2,3584,1024]{2,1,0:T(8,128)(2,1)} %in_ref.3), custom_call_target="tpu_custom_call" | custom-call | bytes 16777216 | tf_op jit(solution)/shard_map/pallas_call | solution.py:139
  34.0 71.3 %all-to-all-done.1 = bf16[16,2,96,1024]{3,2,1,0:T(8,128)(2,1)} async-done(((bf16[16,2,96,1024]{3,2,1,0:T(8,128)(2,1)}), bf16[16,2,96,1024]{3,2,1,0:T(8,128)(2,1)}, u32[]{:S(2)}, u32[]{:S(2)}) %all-to-all-start.1) | async-done | bytes 6291488 | tf_op jit(solution)/shard_map/all_to_all | solution.py:255
  105.4 4.7 all-to-all-start.4
  112.0 0.7 and_and_fusion
  112.9 1.3 add_select_fusion.54
  115.1 122.9 %all-gather.2.cloned.1.call-done = bf16[512,3712]{1,0:T(8,128)(2,1)} async-done(((bf16[16,3712]{1,0:T(8,128)(2,1)}), bf16[512,3712]{1,0:T(8,128)(2,1)}) %all-gather.2.cloned.1.call-update) | async-done | bytes 3801104 | tf_op jit(solution)/shard_map/all_gather | solution.py:277
  238.0 139.8 %conditional.2 = (bf16[16,96,1024]{2,1,0:T(8,128)(2,1)}, bf16[256,1024]{1,0:T(8,128)(2,1)}) conditional(s32[]{:T(128)} %clamp.4, (s32[16]{0:T(128)S(1)}, bf16[32,96,1024]{2,1,0:T(8,128)(2,1)}, bf16[512,3712]{1,0:T(8,128)(2,1)}, s32[32]{0:T(128)}, s32[]{:T(128)}, /*index=5*/s32[32]{0:T(128)S(1)}, ...), branch_computations={%region_4.10_spmd, %region_10.16_spmd, %region_16.22_spmd, %region... | conditional | flops 4735464448 | bytes 61905752 | solution.py:201
  258.8 3.2 branch_12_fun.5
  261.9 2.0 collective-permute-start.27
  264.0 0.9 slice.221
  265.5 0.8 compare_reduce_fusion.12
  266.4 0.8 fusion.120
  267.2 0.7 convert_reduce_fusion.12
  269.7 0.8 reshape.3732.s_ref
  270.5 4.5 convolution_convert_fusion.12.x_ref
  275.0 13.0 %branch_12_fun.7 = bf16[256,1024]{1,0:T(8,128)(2,1)} custom-call(bf16[256,3712]{1,0:T(8,128)(2,1)} %convolution_convert_fusion.12.x_ref, bf16[2,3584,1024]{2,1,0:T(8,128)(2,1)} %get-tuple-element.536.q_ref, f32[2,7,4,1024]{3,2,1,0:T(4,128)} %reshape.3732.s_ref), custom_call_target="tpu_custom_call" | custom-call | flops 3758096384 | bytes 17039360 | tf_op jit(solution)/shard_map/cond/branch_12_fun/pallas_call | solution.py:52
  288.0 79.1 %collective-permute-done.27.far_ref = bf16[12,96,1024]{2,1,0:T(8,128)(2,1)S(1)} collective-permute-done((bf16[12,96,1024]{2,1,0:T(8,128)(2,1)}, bf16[12,96,1024]{2,1,0:T(8,128)(2,1)S(1)}, u32[]{:S(2)}, u32[]{:S(2)}) %collective-permute-start.27) | collective-permute-done | bytes 2359328 | tf_op jit(solution)/shard_map/cond/branch_12_fun/ppermute | solution.py:194
  367.1 1.4 copy-done.11
  368.5 3.7 branch_12_fun.6
  377.9 4.1 all-to-all-start.2
  382.0 155.9 %conditional.3 = (bf16[16,128,1024]{2,1,0:T(8,128)(2,1)}) conditional(s32[]{:T(128)} %clamp.4, (s32[16]{0:T(128)S(1)}, bf16[32,128,1024]{2,1,0:T(8,128)(2,1)}) %tuple.133, (s32[16]{0:T(128)S(1)}, bf16[32,128,1024]{2,1,0:T(8,128)(2,1)}, s32[16]{0:T(128)S(1)}) %tuple.134, (s32[16]{0:T(128)S(1)}, ...), branch_computations={%region_106.107_spmd, %region_107.108_spmd, %region_108.109_spmd, ... | conditional | bytes 47710284 | solution.py:201
  382.0 3.4 branch_12_fun.8
  385.4 3.5 collective-permute-start.11
  388.9 142.8 %collective-permute-done.11.far_ref = bf16[12,128,1024]{2,1,0:T(8,128)(2,1)S(1)} collective-permute-done((bf16[12,128,1024]{2,1,0:T(8,128)(2,1)}, bf16[12,128,1024]{2,1,0:T(8,128)(2,1)S(1)}, u32[]{:S(2)}, u32[]{:S(2)}) %collective-permute-start.11) | collective-permute-done | bytes 3145760 | tf_op jit(solution)/shard_map/cond/branch_12_fun/ppermute | solution.py:194
  531.7 1.8 copy-done.5
  533.4 4.4 branch_12_fun.9
  537.9 4.5 all-to-all-start.5
  542.5 52.6 %all-to-all-done.5.blocks_ref = bf16[16,128,1024]{2,1,0:T(8,128)(2,1)} async-done(((bf16[16,128,1024]{2,1,0:T(8,128)(2,1)}), bf16[16,128,1024]{2,1,0:T(8,128)(2,1)}, u32[]{:S(2)}, u32[]{:S(2)}) %all-to-all-start.5) | async-done | bytes 4194336 | tf_op jit(solution)/shard_map/all_to_all | solution.py:330
  595.1 3.7 all-to-all-start.3
  599.9 0.7 compare_reduce_fusion.18
  600.7 0.7 fusion.187
  602.6 0.9 slice.260
  603.6 0.8 copy.1015
  604.4 0.8 convert_bitcast_fusion
  605.6 0.8 fusion.172
  606.5 0.8 compare_reduce_fusion.17
  607.5 0.7 convert_reduce_fusion.17
  609.2 1.6 convert_reduce_fusion.20
  610.7 2.4 add_bitcast_fusion
  613.1 2.0 fusion.171
  615.1 3.9 shard_map.104.refs_0_
  619.0 19.8 %all-to-all-done.3.blocks_ref = bf16[16,96,1024]{2,1,0:T(8,128)(2,1)S(1)} async-done(((bf16[16,96,1024]{2,1,0:T(8,128)(2,1)}), bf16[16,96,1024]{2,1,0:T(8,128)(2,1)S(1)}, u32[]{:S(2)}, u32[]{:S(2)}) %all-to-all-start.3) | async-done | bytes 3145760 | tf_op jit(solution)/shard_map/all_to_all | solution.py:350
  638.8 1.7 copy-done
  640.4 3.2 shard_map.105
  (87 shorter events, 9.2 us)
Async XLA Ops:
  8.4 14.3 %all-to-all-start = ((bf16[32,1,128]{2,1,0:T(2,128)(2,1)}), bf16[32,1,128]{2,1,0:T(2,128)(2,1)S(1)}, u32[]{:S(2)}, u32[]{:S(2)}) async-start(bf16[32,1,128]{2,1,0:T(2,128)(2,1)} %broadcast_in_dim.632), calls=%async_computation | async-start | bytes 32768 | tf_op jit(solution)/shard_map/all_to_all | solution.py:241
  22.8 82.6 %all-to-all-start.1 = ((bf16[16,2,96,1024]{3,2,1,0:T(8,128)(2,1)}), bf16[16,2,96,1024]{3,2,1,0:T(8,128)(2,1)}, u32[]{:S(2)}, u32[]{:S(2)}) async-start(bf16[16,2,96,1024]{3,2,1,0:T(8,128)(2,1)} %shard_map.103), calls=%async_computation.1 | async-start | bytes 12582912 | tf_op jit(solution)/shard_map/all_to_all | solution.py:255
  34.0 76.2 %copy-start.21 = (bf16[2,28,8]{1,2,0:T(8,128)(2,1)S(1)}, bf16[2,28,8]{1,2,0:T(8,128)(2,1)}, u32[]{:S(2)}) copy-start(bf16[2,28,8]{1,2,0:T(8,128)(2,1)} %param.42) | copy-start | bytes 2692
  34.0 76.4 %copy-start.34 = (s32[16,8]{0,1:T(8,128)S(1)}, s32[16,8]{0,1:T(8,128)}, u32[]{:S(2)}) copy-start(s32[16,8]{0,1:T(8,128)} %param.45) | copy-start | bytes 1540
  34.0 76.5 %copy-start.36 = (s32[16,8]{0,1:T(8,128)S(1)}, s32[16,8]{0,1:T(8,128)}, u32[]{:S(2)}) copy-start(s32[16,8]{0,1:T(8,128)} %param.46) | copy-start | bytes 1540
  34.0 76.6 %copy-start.33 = (bf16[16,3584]{1,0:T(8,128)(2,1)S(1)}, bf16[16,3584]{1,0:T(8,128)(2,1)}, u32[]{:S(2)}) copy-start(bf16[16,3584]{1,0:T(8,128)(2,1)} %param.44) | copy-start | bytes 344068
  105.4 272.5 %all-to-all-start.4 = ((bf16[16,2,128,1024]{3,2,1,0:T(8,128)(2,1)}), bf16[16,2,128,1024]{3,2,1,0:T(8,128)(2,1)}, u32[]{:S(2)}, u32[]{:S(2)}) async-start(bf16[16,2,128,1024]{3,2,1,0:T(8,128)(2,1)} %shard_map.102), calls=%async_computation.4 | async-start | bytes 16777216 | tf_op jit(solution)/shard_map/all_to_all | solution.py:255
  110.1 127.9 %all-gather.2.cloned.1.call-start = ((), (), s32[]{:S(2)}) async-start(), calls=%async_computation.6 | async-start | bytes 3919872 | tf_op jit(solution)/shard_map/all_gather | solution.py:277
  261.9 105.2 %collective-permute-start.27 = (bf16[12,96,1024]{2,1,0:T(8,128)(2,1)}, bf16[12,96,1024]{2,1,0:T(8,128)(2,1)S(1)}, u32[]{:S(2)}, u32[]{:S(2)}) collective-permute-start(bf16[12,96,1024]{2,1,0:T(8,128)(2,1)} %branch_12_fun.5), channel_id=1, source_target_pairs={{0,4},{1,5},{2,6},{3,7},{4,0},{5,1},{6,2},{7,3},{8,12},{9,13},{10,... | collective-permute-start | bytes 7077896 | tf_op jit(solution)/shard_map/cond/branch_12_fun/ppermute | solution.py:194
  367.1 1.4 copy-start.11
  377.9 160.0 %all-to-all-start.2 = ((bf16[32,8,1024]{2,1,0:T(8,128)(2,1)}), bf16[32,8,1024]{2,1,0:T(8,128)(2,1)}, u32[]{:S(2)}, u32[]{:S(2)}) async-start(bf16[32,8,1024]{2,1,0:T(8,128)(2,1)} %bitcast.70), calls=%async_computation.2 | async-start | bytes 1048576 | tf_op jit(solution)/shard_map/all_to_all | solution.py:342
  385.4 146.3 %collective-permute-start.11 = (bf16[12,128,1024]{2,1,0:T(8,128)(2,1)}, bf16[12,128,1024]{2,1,0:T(8,128)(2,1)S(1)}, u32[]{:S(2)}, u32[]{:S(2)}) collective-permute-start(bf16[12,128,1024]{2,1,0:T(8,128)(2,1)} %branch_12_fun.8), channel_id=1, source_target_pairs={{0,4},{1,5},{2,6},{3,7},{4,0},{5,1},{6,2},{7,3},{8,12},{9,13},{10,... | collective-permute-start | bytes 9437192 | tf_op jit(solution)/shard_map/cond/branch_12_fun/ppermute | solution.py:194
  531.7 1.8 copy-start.5
  537.9 57.2 %all-to-all-start.5 = ((bf16[16,128,1024]{2,1,0:T(8,128)(2,1)}), bf16[16,128,1024]{2,1,0:T(8,128)(2,1)}, u32[]{:S(2)}, u32[]{:S(2)}) async-start(bf16[16,128,1024]{2,1,0:T(8,128)(2,1)} %get-tuple-element.1813), calls=%async_computation.5 | async-start | bytes 8388608 | tf_op jit(solution)/shard_map/all_to_all | solution.py:330
  542.5 56.4 %copy-start.35 = (s32[16,8]{0,1:T(8,128)S(1)}, s32[16,8]{0,1:T(8,128)}, u32[]{:S(2)}) copy-start(s32[16,8]{0,1:T(8,128)} %param.45) | copy-start | bytes 1540
  542.5 56.5 %copy-start.37 = (s32[16,8]{0,1:T(8,128)S(1)}, s32[16,8]{0,1:T(8,128)}, u32[]{:S(2)}) copy-start(s32[16,8]{0,1:T(8,128)} %param.46) | copy-start | bytes 1540
  542.5 56.7 %copy-start.38 = (s32[16,8]{0,1:T(8,128)S(1)}, s32[16,8]{0,1:T(8,128)}, u32[]{:S(2)}) copy-start(s32[16,8]{0,1:T(8,128)} %param.47) | copy-start | bytes 1540
  595.1 43.7 %all-to-all-start.3 = ((bf16[16,96,1024]{2,1,0:T(8,128)(2,1)}), bf16[16,96,1024]{2,1,0:T(8,128)(2,1)S(1)}, u32[]{:S(2)}, u32[]{:S(2)}) async-start(bf16[16,96,1024]{2,1,0:T(8,128)(2,1)} %get-tuple-element.638), calls=%async_computation.3 | async-start | bytes 6291456 | tf_op jit(solution)/shard_map/all_to_all | solution.py:350
  638.8 1.7 copy-start
Sparse Core Ops, SparseCore 0:
  114.4 123.5 all-gather.1
where the time goes:
time: 659 us; the launch traced here: 651 us
  waiting for transfers between devices  490 us (74%)
  Pallas kernels  46.8 us (7%)
  starting transfers between devices  34.6 us (5%)
  loops' own time  26.5 us (4%)
  other arithmetic  17.4 us (3%)
  between operations  16.2 us (2%)
  local copies, waits for them, and re-layouts  12.8 us (2%)
    ppermute x2, waiting for transfers between devices, branch(): arrived = lax.ppermute(gather(leave_rows[:size], block, block), AXES, pairs)  222 us
    all_gather x1, waiting for transfers between devices, per_device(): held = lax.all_gather(held, AXES, axis=0, tiled=True)  123 us
    all_to_all x2, waiting for transfers between devices, per_device(): lax.all_to_all(block, AXES, split_axis=0, concat_axis=0, tiled=True, axis...  71.3 us
    all_to_all x1, waiting for transfers between devices, per_device(): lax.all_to_all(first, AXES, split_axis=0, concat_axis=0, tiled=True, axis...  52.6 us
    another operation x2, loops' own time, cross_over(): return lax.switch(count, branches, leave_rows, give_rows, block, *operands)  26.5 us
    all_to_all x1, waiting for transfers between devices, per_device(): lax.all_to_all(second, AXES, split_axis=0, concat_axis=0, tiled=True, axi...  19.8 us
    pallas_call x4, Pallas kernels, gather(): pl.pallas_call(gather_kernel, in_specs=[pl.BlockSpec(memory_space=pltpu.S...  14.7 us
  transfers between devices with their start and end apart: 9, of which 7 were waited for; matrix products, arithmetic and copies ran while one was open for 5% of the time, Pallas kernels for 7%

commit v1 on v0

--- a/solution.py
+++ b/solution.py
@@ -10,6 +10,7 @@
 TILE = 128
 CAP = 2
 POOL = 16
+COMMON = 8
 VMEM_LIMIT = 60 * 1024 * 1024
 AXES = ("group", "dev")
 PARTS = (128, 96)
@@ -81,32 +82,36 @@
         pl.loop(0, count)(stage)
 
 
-def gather_kernel(index_ref, near_ref, far_ref, out_ref, held, in_sem, out_sem):
-    near_count = near_ref.shape[0]
+def gather_kernel(index_ref, *refs):
+    *source_refs, out_ref, held, in_sem, out_sem = refs
 
     def start(spot):
         index = index_ref[spot]
-
-        @pl.when(index < near_count)
-        def _():
-            near_index = jnp.minimum(index, near_count - 1)
-            pltpu.make_async_copy(near_ref.at[near_index], held.at[spot], in_sem.at[spot]).start()
-
-        @pl.when(index >= near_count)
-        def _():
-            far_index = jnp.clip(index - near_count, 0, far_ref.shape[0] - 1)
-            pltpu.make_async_copy(far_ref.at[far_index], held.at[spot], in_sem.at[spot]).start()
+        base = 0
+        for source_ref in source_refs:
+            count = source_ref.shape[0]
+            inside = (index >= base) & (index < base + count)
+            at = jnp.clip(index - base, 0, count - 1)
+
+            @pl.when(inside)
+            def _():
+                pltpu.make_async_copy(
+                    source_ref.at[at], held.at[spot], in_sem.at[spot]
+                ).start()
+
+            base += count
 
     through_vmem(out_ref.shape[0], start, lambda spot: out_ref.at[spot], held, in_sem, out_sem)
 
 
-def gather(indices, near, far):
+def gather(indices, *sources):
     count = indices.shape[0]
+    indices = jnp.clip(indices, 0, sum(source.shape[0] for source in sources) - 1)
     anywhere = pl.BlockSpec(memory_space=pl.ANY)
-    out = jax.ShapeDtypeStruct((count,) + near.shape[1:], near.dtype)
+    out = jax.ShapeDtypeStruct((count,) + sources[0].shape[1:], sources[0].dtype)
     return pl.pallas_call(
         gather_kernel,
-        in_specs=[pl.BlockSpec(memory_space=pltpu.SMEM), anywhere, anywhere],
+        in_specs=[pl.BlockSpec(memory_space=pltpu.SMEM)] + [anywhere] * len(sources),
         out_specs=anywhere,
         out_shape=out,
         scratch_shapes=[
@@ -115,10 +120,8 @@
             pltpu.SemaphoreType.DMA((count,)),
         ],
         compiler_params=pltpu.CompilerParams(vmem_limit_bytes=VMEM_LIMIT),
-        cost_estimate=pl.CostEstimate(
-            flops=0, bytes_accessed=4 * out.size, transcendentals=0
-        ),
-    )(indices, near, far)
+        cost_estimate=pl.CostEstimate(flops=0, bytes_accessed=4 * out.size, transcendentals=0),
+    )(indices, *sources)
 
 
 def chunk_kernel(first, in_ref, out_ref, held, in_sem, out_sem):
@@ -186,19 +189,23 @@
     )(*operands)
 
 
-def cross_over(count, leave_rows, give_rows, block, pairs, beside=None, operands=()):
+def start_over(leave_rows, block, pairs):
+    return lax.ppermute(gather(leave_rows[:COMMON], block), AXES, pairs)
+
+
+def cross_over(count, leave_rows, give_rows, block, common, pairs):
     def branch_of(size):
-        def branch(leave_rows, give_rows, block, *operands):
-            arrived = block
-            if size > 0:
-                arrived = lax.ppermute(gather(leave_rows[:size], block, block), AXES, pairs)
-            extra = () if beside is None else (beside(*operands),)
-            return (gather(give_rows, block, arrived),) + extra
+        def branch(leave_rows, give_rows, block, common):
+            if size == 0:
+                return gather(give_rows, block, common)
+            late = gather(leave_rows[COMMON : COMMON + size], block)
+            return gather(give_rows, block, common, lax.ppermute(late, AXES, pairs))
 
         return branch
 
-    branches = [branch_of(size) for size in range(POOL + 1)]
-    return lax.switch(count, branches, leave_rows, give_rows, block, *operands)
+    branches = [branch_of(size) for size in range(POOL - COMMON + 1)]
+    size = jnp.maximum(count - COMMON, 0)
+    return lax.switch(size, branches, leave_rows, give_rows, block, common)
 
 
 def route(experts, replica, place_all, holding):
@@ -326,19 +333,14 @@
         axis=1,
     )
     first, second = spread
-    (first,) = cross_over(cross_count, leave_rows, give_rows, first, over)
+    common = start_over(leave_rows, first, over)
+    first = cross_over(cross_count, leave_rows, give_rows, first, common, over)
+    first, leave_rows, held = lax.optimization_barrier((first, leave_rows, held))
     first = lax.all_to_all(
         first, AXES, split_axis=0, concat_axis=0, tiled=True, axis_index_groups=pools
     )
-    second, activated = cross_over(
-        cross_count,
-        leave_rows,
-        give_rows,
-        second,
-        over,
-        work,
-        (held, place_all, primary_q, primary_scales),
-    )
+    common = start_over(leave_rows, second, over)
+    activated = work(held, place_all, primary_q, primary_scales)
     returned = lax.all_to_all(
         activated.reshape(device_count, holding * cells, hidden),
         AXES,
@@ -346,7 +348,9 @@
         concat_axis=0,
         tiled=True,
     )
-    second, returned, held = lax.optimization_barrier((second, returned, held))
+    common, returned = lax.optimization_barrier((common, returned))
+    second = cross_over(cross_count, leave_rows, give_rows, second, common, over)
+    second, held = lax.optimization_barrier((second, held))
     second = lax.all_to_all(
         second, AXES, split_axis=0, concat_axis=0, tiled=True, axis_index_groups=pools
     )

time: 659 us -> 504 us (0.76); the launches traced: 651 us -> 503 us
  waiting for transfers between devices: 490 us -> 344 us
  loops' own time: 26.5 us -> 1.37 us
  blocking collectives: 0 us -> 22.9 us
    all_gather x1, waiting for transfers between devices: 123 us -> 0.02 us  [per_device(): held = lax.all_gather(held, AXES, axis=0, tiled=True)]
    all_to_all x1, waiting for transfers between devices: 52.6 us -> 0.01 us  [per_device(): lax.all_to_all(first, AXES, split_axis=0, concat_axis=0, tiled=True, axis...]
    all_to_all x2, waiting for transfers between devices: 71.3 us -> 97.7 us  [per_device(): lax.all_to_all(block, AXES, split_axis=0, concat_axis=0, tiled=True, axis...]
    another operation x2, loops' own time: 26.5 us -> 1.37 us  [cross_over(): return lax.switch(size, branches, leave_rows, give_rows, block, common)]
    all_to_all x0 -> x1, blocking collectives: none -> 22.9 us  [per_device(): lax.all_to_all(activated.reshape(device_count, holding * cells, hidden),...]
    pallas_call x4 -> x6, Pallas kernels: 14.7 us -> 18.6 us  [gather(): pl.pallas_call(gather_kernel, in_specs=[pl.BlockSpec(memory_space=pltpu.S...]
    ppermute x2 -> x4, waiting for transfers between devices: 222 us -> 224 us  [the longest x2 196 us: start_over(): return lax.ppermute(gather(leave_rows[:COMMON], block), AXES, pairs)]
  transfers between devices with their start and end apart: 9 -> 10, of which waited for: 7 -> 7; matrix products, arithmetic and copies ran while one was open for 5% -> 6% of each run, Pallas kernels for 7% -> 9%
where the time goes in v1:
time: 504 us; the launch traced here: 503 us
  waiting for transfers between devices  344 us (68%)
  Pallas kernels  50.7 us (10%)
  starting transfers between devices  34.2 us (7%)
  blocking collectives  22.9 us (5%)
  between operations  15.8 us (3%)
  other arithmetic  15.1 us (3%)
  local copies, waits for them, and re-layouts  12.1 us (2%)
  matrix products  6.61 us (1%)
    ppermute x2, waiting for transfers between devices, start_over(): return lax.ppermute(gather(leave_rows[:COMMON], block), AXES, pairs)  196 us
    all_to_all x2, waiting for transfers between devices, per_device(): lax.all_to_all(block, AXES, split_axis=0, concat_axis=0, tiled=True, axis...  97.7 us
    ppermute x2, waiting for transfers between devices, branch(): return gather(give_rows, block, common, lax.ppermute(late, AXES, pairs))  28.2 us
    all_to_all x1, blocking collectives, per_device(): lax.all_to_all(activated.reshape(device_count, holding * cells, hidden),...  22.9 us
    all_to_all x1, waiting for transfers between devices, per_device(): lax.all_to_all(second, AXES, split_axis=0, concat_axis=0, tiled=True, axi...  21.6 us
    pallas_call x6, Pallas kernels, gather(): pl.pallas_call(gather_kernel, in_specs=[pl.BlockSpec(memory_space=pltpu.S...  18.6 us
    pallas_call x1, Pallas kernels, serve(): pl.pallas_call(expert_kernel, grid=(steps,), in_specs=[pl.BlockSpec((coun...  13 us
    pallas_call x2, Pallas kernels, by_chunk(): pl.pallas_call(functools.partial(chunk_kernel, first), in_specs=[anywhere...  12.1 us
  transfers between devices with their start and end apart: 10, of which 7 were waited for; matrix products, arithmetic and copies ran while one was open for 6% of the time, Pallas kernels for 9%

profile of v1, /device:TPU:0, one launch (start us, length us, event | category | flops | bytes accessed | tf_op | source)
XLA Modules:
  0.0 503.1 jit_solution(4542316008766772462)
XLA Ops:
  8.4 7.3 %all-to-all-start = ((bf16[32,1,128]{2,1,0:T(2,128)(2,1)}), bf16[32,1,128]{2,1,0:T(2,128)(2,1)S(1)}, u32[]{:S(2)}, u32[]{:S(2)}) async-start(bf16[32,1,128]{2,1,0:T(2,128)(2,1)} %broadcast_in_dim.66), calls=%async_computation | async-start | bytes 32768 | tf_op jit(solution)/shard_map/all_to_all | solution.py:248
  15.7 6.6 %shard_map.102 = bf16[16,2,128,1024]{3,2,1,0:T(8,128)(2,1)} custom-call(bf16[2,3584,1024]{2,1,0:T(8,128)(2,1)} %q_ref.1), custom_call_target="tpu_custom_call" | custom-call | bytes 16777216 | tf_op jit(solution)/shard_map/pallas_call | solution.py:142
  22.8 4.7 all-to-all-start.2
  27.5 5.5 %shard_map.103 = bf16[16,2,96,1024]{3,2,1,0:T(8,128)(2,1)} custom-call(bf16[2,3584,1024]{2,1,0:T(8,128)(2,1)} %q_ref.1), custom_call_target="tpu_custom_call" | custom-call | bytes 12582912 | tf_op jit(solution)/shard_map/pallas_call | solution.py:142
  33.1 97.7 %all-to-all-done.2 = bf16[16,2,128,1024]{3,2,1,0:T(8,128)(2,1)} async-done(((bf16[16,2,128,1024]{3,2,1,0:T(8,128)(2,1)}), bf16[16,2,128,1024]{3,2,1,0:T(8,128)(2,1)}, u32[]{:S(2)}, u32[]{:S(2)}) %all-to-all-start.2) | async-done | bytes 8388640 | tf_op jit(solution)/shard_map/all_to_all | solution.py:262
  130.8 4.7 all-to-all-start.1
  136.0 0.7 pad_maximum_fusion
  137.1 0.6 add_select_fusion.6
  138.4 3.1 shard_map.104
  141.4 2.4 collective-permute-start.16
  144.5 0.8 reshape_reshape.3.s_ref
  146.3 116.0 %collective-permute-done.16 = bf16[8,128,1024]{2,1,0:T(8,128)(2,1)S(1)} collective-permute-done((bf16[8,128,1024]{2,1,0:T(8,128)(2,1)}, bf16[8,128,1024]{2,1,0:T(8,128)(2,1)S(1)}, u32[]{:S(2)}, u32[]{:S(2)}) %collective-permute-start.16) | collective-permute-done | bytes 2097184 | tf_op jit(solution)/shard_map/ppermute | solution.py:193
  262.3 31.7 %conditional.2 = (bf16[16,128,1024]{2,1,0:T(8,128)(2,1)}) conditional(s32[]{:T(128)} %clamp.38, (s32[16]{0:T(128)S(1)}, bf16[32,128,1024]{2,1,0:T(8,128)(2,1)}, bf16[8,128,1024]{2,1,0:T(8,128)(2,1)S(1)}) %tuple.67, (s32[16]{0:T(128)S(1)}, s32[16]{0:T(128)S(1)}, bf16[32,128,1024]{2,1,0:T(8,128)(2,1)}, ...), branch_computations={%region_4.5_spmd, %region_5.6_spmd, %region_6.7_spmd, %region_7.8_... | conditional | flops 24 | bytes 21496052 | solution.py:208
  263.5 1.7 branch_1_fun.4
  265.2 3.3 collective-permute-start
  269.1 19.7 %collective-permute-done.refs_2_ = bf16[1,128,1024]{2,1,0:T(8,128)(2,1)S(1)} collective-permute-done((bf16[1,128,1024]{2,1,0:T(8,128)(2,1)}, bf16[1,128,1024]{2,1,0:T(8,128)(2,1)S(1)}, u32[]{:S(2)}, u32[]{:S(2)}) %collective-permute-start) | collective-permute-done | bytes 262176 | tf_op jit(solution)/shard_map/cond/branch_1_fun/ppermute | solution.py:202
  288.7 0.7 copy-done.12
  289.4 4.5 branch_1_fun.5
  294.0 0.9 slice.82
  295.9 0.7 convert_reduce_fusion.1
  296.7 0.6 fusion.7
  298.1 4.6 convolution_convert_fusion.x_ref
  302.7 13.0 %shard_map.106 = bf16[256,1024]{1,0:T(8,128)(2,1)} custom-call(bf16[256,3712]{1,0:T(8,128)(2,1)} %convolution_convert_fusion.x_ref, bf16[2,3584,1024]{2,1,0:T(8,128)(2,1)} %q_ref.1, f32[2,7,4,1024]{3,2,1,0:T(4,128)} %reshape_reshape.3.s_ref), custom_call_target="tpu_custom_call" | custom-call | flops 3758096384 | bytes 17039360 | tf_op jit(solution)/shard_map/pallas_call | solution.py:53
  315.7 22.9 %all_to_all.34 = bf16[32,8,1024]{2,1,0:T(8,128)(2,1)} all-to-all(bf16[32,8,1024]{2,1,0:T(8,128)(2,1)} %bitcast.52), channel_id=1, replica_groups=mesh['group'=4,'dev'=8] {'group','dev'}, dimensions={0} | all-to-all | bytes 1048576 | tf_op jit(solution)/shard_map/all_to_all | solution.py:344
  338.7 4.5 all-to-all-start.5
  343.7 3.0 shard_map.105
  346.8 80.2 %collective-permute-done.17 = bf16[8,96,1024]{2,1,0:T(8,128)(2,1)S(1)} collective-permute-done((bf16[8,96,1024]{2,1,0:T(8,128)(2,1)}, bf16[8,96,1024]{2,1,0:T(8,128)(2,1)S(1)}, u32[]{:S(2)}, u32[]{:S(2)}) %collective-permute-start.17) | collective-permute-done | bytes 1572896 | tf_op jit(solution)/shard_map/ppermute | solution.py:193
  427.0 20.7 %conditional.3 = (bf16[16,96,1024]{2,1,0:T(8,128)(2,1)}) conditional(s32[]{:T(128)} %clamp.38, (s32[16]{0:T(128)S(1)}, bf16[32,96,1024]{2,1,0:T(8,128)(2,1)}, bf16[8,96,1024]{2,1,0:T(8,128)(2,1)S(1)}) %tuple.71, (s32[16]{0:T(128)S(1)}, s32[16]{0:T(128)S(1)}, bf16[32,96,1024]{2,1,0:T(8,128)(2,1)}, ...), branch_computations={%region_18.19_spmd, %region_19.20_spmd, %region_20.21_spmd, %regio... | conditional | flops 24 | bytes 22020364 | solution.py:208
  428.2 1.6 branch_1_fun.6
  429.8 3.3 collective-permute-start.8
  433.7 8.5 %collective-permute-done.8.refs_2_ = bf16[1,96,1024]{2,1,0:T(8,128)(2,1)S(1)} collective-permute-done((bf16[1,96,1024]{2,1,0:T(8,128)(2,1)}, bf16[1,96,1024]{2,1,0:T(8,128)(2,1)S(1)}, u32[]{:S(2)}, u32[]{:S(2)}) %collective-permute-start.8) | collective-permute-done | bytes 196640 | tf_op jit(solution)/shard_map/cond/branch_1_fun/ppermute | solution.py:202
  442.2 0.7 copy-done.13
  442.9 4.8 branch_1_fun.7
  447.7 3.8 all-to-all-start.4
  453.4 0.9 slice.85
  454.4 0.8 copy.165
  455.2 0.8 convert_bitcast_fusion
  456.3 0.8 fusion.3
  457.2 0.8 compare_reduce_fusion
  458.2 0.7 convert_reduce_fusion
  459.2 0.7 copy.160
  459.9 1.6 convert_reduce_fusion.4
  461.5 2.5 add_bitcast_fusion
  463.9 2.0 fusion.1
  465.9 3.9 shard_map.107.refs_0_
  469.8 21.6 %all-to-all-done.4.blocks_ref = bf16[16,96,1024]{2,1,0:T(8,128)(2,1)S(1)} async-done(((bf16[16,96,1024]{2,1,0:T(8,128)(2,1)}), bf16[16,96,1024]{2,1,0:T(8,128)(2,1)S(1)}, u32[]{:S(2)}, u32[]{:S(2)}) %all-to-all-start.4) | async-done | bytes 3145760 | tf_op jit(solution)/shard_map/all_to_all | solution.py:354
  491.4 1.6 copy-done
  493.0 3.2 shard_map.108
  (92 shorter events, 11.0 us)
Async XLA Ops:
  8.4 14.3 %all-to-all-start = ((bf16[32,1,128]{2,1,0:T(2,128)(2,1)}), bf16[32,1,128]{2,1,0:T(2,128)(2,1)S(1)}, u32[]{:S(2)}, u32[]{:S(2)}) async-start(bf16[32,1,128]{2,1,0:T(2,128)(2,1)} %broadcast_in_dim.66), calls=%async_computation | async-start | bytes 32768 | tf_op jit(solution)/shard_map/all_to_all | solution.py:248
  22.8 108.0 %all-to-all-start.2 = ((bf16[16,2,128,1024]{3,2,1,0:T(8,128)(2,1)}), bf16[16,2,128,1024]{3,2,1,0:T(8,128)(2,1)}, u32[]{:S(2)}, u32[]{:S(2)}) async-start(bf16[16,2,128,1024]{3,2,1,0:T(8,128)(2,1)} %shard_map.102), calls=%async_computation.2 | async-start | bytes 16777216 | tf_op jit(solution)/shard_map/all_to_all | solution.py:262
  33.1 102.4 %copy-start.16 = (bf16[2,28,8]{1,2,0:T(8,128)(2,1)S(1)}, bf16[2,28,8]{1,2,0:T(8,128)(2,1)}, u32[]{:S(2)}) copy-start(bf16[2,28,8]{1,2,0:T(8,128)(2,1)} %param.26) | copy-start | bytes 2692
  33.1 102.6 %copy-start.17 = (s32[16,8]{0,1:T(8,128)S(1)}, s32[16,8]{0,1:T(8,128)}, u32[]{:S(2)}) copy-start(s32[16,8]{0,1:T(8,128)} %param.29) | copy-start | bytes 1540
  33.1 102.7 %copy-start.18 = (s32[16,8]{0,1:T(8,128)S(1)}, s32[16,8]{0,1:T(8,128)}, u32[]{:S(2)}) copy-start(s32[16,8]{0,1:T(8,128)} %param.30) | copy-start | bytes 1540
  33.1 102.9 %copy-start.14 = (bf16[16,3584]{1,0:T(8,128)(2,1)S(1)}, bf16[16,3584]{1,0:T(8,128)(2,1)}, u32[]{:S(2)}) copy-start(bf16[16,3584]{1,0:T(8,128)(2,1)} %param.28) | copy-start | bytes 344068
  130.8 185.0 %all-to-all-start.1 = ((bf16[16,2,96,1024]{3,2,1,0:T(8,128)(2,1)}), bf16[16,2,96,1024]{3,2,1,0:T(8,128)(2,1)}, u32[]{:S(2)}, u32[]{:S(2)}) async-start(bf16[16,2,96,1024]{3,2,1,0:T(8,128)(2,1)} %shard_map.103), calls=%async_computation.1 | async-start | bytes 12582912 | tf_op jit(solution)/shard_map/all_to_all | solution.py:262
  135.5 158.5 %all-gather.2.cloned.1.call-start = ((), (), s32[]{:S(2)}) async-start(), calls=%async_computation.6 | async-start | bytes 3919872 | tf_op jit(solution)/shard_map/all_gather | solution.py:284
  136.9 158.9 %copy-start.15 = (s32[32]{0:T(128)}, s32[32]{0:T(128)S(1)}, u32[]{:S(2)}) copy-start(s32[32]{0:T(128)S(1)} %convert_reduce_fusion.6) | copy-start | bytes 388
  141.4 120.8 %collective-permute-start.16 = (bf16[8,128,1024]{2,1,0:T(8,128)(2,1)}, bf16[8,128,1024]{2,1,0:T(8,128)(2,1)S(1)}, u32[]{:S(2)}, u32[]{:S(2)}) collective-permute-start(bf16[8,128,1024]{2,1,0:T(8,128)(2,1)} %shard_map.104), channel_id=1, source_target_pairs={{0,4},{1,5},{2,6},{3,7},{4,0},{5,1},{6,2},{7,3},{8,12},{9,13},{10,... | collective-permute-start | bytes 6291464 | tf_op jit(solution)/shard_map/ppermute | solution.py:193
  265.2 23.5 %collective-permute-start = (bf16[1,128,1024]{2,1,0:T(8,128)(2,1)}, bf16[1,128,1024]{2,1,0:T(8,128)(2,1)S(1)}, u32[]{:S(2)}, u32[]{:S(2)}) collective-permute-start(bf16[1,128,1024]{2,1,0:T(8,128)(2,1)} %branch_1_fun.4), channel_id=1, source_target_pairs={{0,4},{1,5},{2,6},{3,7},{4,0},{5,1},{6,2},{7,3},{8,12},{9,13},{10,... | collective-permute-start | bytes 786440 | tf_op jit(solution)/shard_map/cond/branch_1_fun/ppermute | solution.py:202
  288.7 0.7 copy-start.12
  338.7 109.0 %all-to-all-start.5 = ((bf16[16,128,1024]{2,1,0:T(8,128)(2,1)}), bf16[16,128,1024]{2,1,0:T(8,128)(2,1)}, u32[]{:S(2)}, u32[]{:S(2)}) async-start(bf16[16,128,1024]{2,1,0:T(8,128)(2,1)} %get-tuple-element.294), calls=%async_computation.5 | async-start | bytes 8388608 | tf_op jit(solution)/shard_map/all_to_all | solution.py:339
  346.7 80.3 %collective-permute-start.17 = (bf16[8,96,1024]{2,1,0:T(8,128)(2,1)}, bf16[8,96,1024]{2,1,0:T(8,128)(2,1)S(1)}, u32[]{:S(2)}, u32[]{:S(2)}) collective-permute-start(bf16[8,96,1024]{2,1,0:T(8,128)(2,1)} %shard_map.105), channel_id=1, source_target_pairs={{0,4},{1,5},{2,6},{3,7},{4,0},{5,1},{6,2},{7,3},{8,12},{9,13},{10,... | collective-permute-start | bytes 4718600 | tf_op jit(solution)/shard_map/ppermute | solution.py:193
  429.8 12.4 %collective-permute-start.8 = (bf16[1,96,1024]{2,1,0:T(8,128)(2,1)}, bf16[1,96,1024]{2,1,0:T(8,128)(2,1)S(1)}, u32[]{:S(2)}, u32[]{:S(2)}) collective-permute-start(bf16[1,96,1024]{2,1,0:T(8,128)(2,1)} %branch_1_fun.6), channel_id=1, source_target_pairs={{0,4},{1,5},{2,6},{3,7},{4,0},{5,1},{6,2},{7,3},{8,12},{9,13},{10,... | collective-permute-start | bytes 589832 | tf_op jit(solution)/shard_map/cond/branch_1_fun/ppermute | solution.py:202
  442.2 0.7 copy-start.13
  447.7 3.8 copy-start.19
  447.7 43.7 %all-to-all-start.4 = ((bf16[16,96,1024]{2,1,0:T(8,128)(2,1)}), bf16[16,96,1024]{2,1,0:T(8,128)(2,1)S(1)}, u32[]{:S(2)}, u32[]{:S(2)}) async-start(bf16[16,96,1024]{2,1,0:T(8,128)(2,1)} %get-tuple-element.295), calls=%async_computation.4 | async-start | bytes 6291456 | tf_op jit(solution)/shard_map/all_to_all | solution.py:354
  491.4 1.6 copy-start
Sparse Core Ops, SparseCore 0:
  139.2 153.5 all-gather.1

commit v2 on v1

--- a/solution.py
+++ b/solution.py
@@ -253,18 +253,6 @@
         tiled=True,
     )
 
-    spread = []
-    start = 0
-    for height in PARTS:
-        block = by_chunk(primary_q, start, height)
-        if not spread:
-            block, place_all = lax.optimization_barrier((block, place_all))
-        block = lax.all_to_all(
-            block, AXES, split_axis=0, concat_axis=0, tiled=True, axis_index_groups=pools
-        )
-        spread.append(block.reshape(POOL * holding, height, hidden))
-        start += POOL * height
-    place_all = place_all[:, 0].astype(jnp.int32)
     device_ids = jnp.arange(device_count, dtype=jnp.int32)
     my_id = first_dev + my_dev
 
@@ -282,6 +270,21 @@
     notice = jnp.pad(notice, ((0, 0), (0, -notice.shape[1] % TILE)))
     held = jnp.concatenate([tokens, notice], axis=1)
     held = lax.all_gather(held, AXES, axis=0, tiled=True)
+
+    def spread_over(block):
+        block = lax.all_to_all(
+            block, AXES, split_axis=0, concat_axis=0, tiled=True, axis_index_groups=pools
+        )
+        return block.reshape((POOL * holding,) + block.shape[2:])
+
+    first_height, second_height = PARTS
+    first, place_all = lax.optimization_barrier((by_chunk(primary_q, 0, first_height), place_all))
+    first = spread_over(first)
+    place_all = place_all[:, 0].astype(jnp.int32)
+    second = by_chunk(primary_q, POOL * first_height, second_height)
+    second, held = lax.optimization_barrier((second, held))
+    second = spread_over(second)
+
     cells = 2 * CAP
     cell_count = device_count * holding * cells
 
@@ -332,15 +335,9 @@
         ),
         axis=1,
     )
-    first, second = spread
     common = start_over(leave_rows, first, over)
-    first = cross_over(cross_count, leave_rows, give_rows, first, common, over)
-    first, leave_rows, held = lax.optimization_barrier((first, leave_rows, held))
-    first = lax.all_to_all(
-        first, AXES, split_axis=0, concat_axis=0, tiled=True, axis_index_groups=pools
-    )
-    common = start_over(leave_rows, second, over)
     activated = work(held, place_all, primary_q, primary_scales)
+    activated, second = lax.optimization_barrier((activated, second))
     returned = lax.all_to_all(
         activated.reshape(device_count, holding * cells, hidden),
         AXES,
@@ -349,6 +346,12 @@
         tiled=True,
     )
     common, returned = lax.optimization_barrier((common, returned))
+    first = cross_over(cross_count, leave_rows, give_rows, first, common, over)
+    first, leave_rows = lax.optimization_barrier((first, leave_rows))
+    first = lax.all_to_all(
+        first, AXES, split_axis=0, concat_axis=0, tiled=True, axis_index_groups=pools
+    )
+    common = start_over(leave_rows, second, over)
     second = cross_over(cross_count, leave_rows, give_rows, second, common, over)
     second, held = lax.optimization_barrier((second, held))
     second = lax.all_to_all(

time: 504 us -> 455 us (0.903)
  blocking collectives: 22.9 us -> 0 us
  waiting for transfers between devices: 344 us -> 335 us
    all_gather x1, waiting for transfers between devices: 0.02 us -> 122 us  [per_device(): held = lax.all_gather(held, AXES, axis=0, tiled=True)]
    ppermute x2, waiting for transfers between devices: 196 us -> 80.1 us  [start_over(): return lax.ppermute(gather(leave_rows[:COMMON], block), AXES, pairs)]
    ppermute x2 -> x0, waiting for transfers between devices: 28.2 us -> none  [branch(): return gather(give_rows, block, common, lax.ppermute(late, AXES, pairs))]
    all_to_all x1 -> x0, blocking collectives: 22.9 us -> none  [per_device(): lax.all_to_all(activated.reshape(device_count, holding * cells, hidden),...]
    all_to_all x2 -> x3, waiting for transfers between devices: 97.7 us -> 107 us  [the longest x2 91.4 us: spread_over(): lax.all_to_all(block, AXES, split_axis=0, concat_axis=0, tiled=True, axis...]
    ppermute x2 -> x0, starting transfers between devices: 6.68 us -> none  [branch(): return gather(give_rows, block, common, lax.ppermute(late, AXES, pairs))]
    pallas_call x6 -> x4, Pallas kernels: 18.6 us -> 14.7 us  [gather(): pl.pallas_call(gather_kernel, in_specs=[pl.BlockSpec(memory_space=pltpu.S...]
    all_to_all x2 -> x3, starting transfers between devices: 9.41 us -> 12.3 us  [the longest x2 9.69 us: spread_over(): lax.all_to_all(block, AXES, split_axis=0, concat_axis=0, tiled=True, axis...]
  transfers between devices with their start and end apart: 10 -> 9, of which waited for: 7 -> 6; matrix products, arithmetic and copies ran while one was open for 6% -> 5% of each run, Pallas kernels for 9% -> 9%
where the time goes in v2:
time: 455 us; the launch traced here: 454 us
  waiting for transfers between devices  335 us (74%)
  Pallas kernels  46.8 us (10%)
  starting transfers between devices  29.4 us (6%)
  between operations  15.8 us (3%)
  other arithmetic  12.6 us (3%)
  local copies, waits for them, and re-layouts  8.28 us (2%)
  matrix products  6.59 us (1%)
    all_gather x1, waiting for transfers between devices, per_device(): held = lax.all_gather(held, AXES, axis=0, tiled=True)  122 us
    all_to_all x2, waiting for transfers between devices, spread_over(): lax.all_to_all(block, AXES, split_axis=0, concat_axis=0, tiled=True, axis...  91.4 us
    ppermute x2, waiting for transfers between devices, start_over(): return lax.ppermute(gather(leave_rows[:COMMON], block), AXES, pairs)  80.1 us
    all_to_all x1, waiting for transfers between devices, per_device(): lax.all_to_all(second, AXES, split_axis=0, concat_axis=0, tiled=True, axi...  25.2 us
    all_to_all x1, waiting for transfers between devices, per_device(): lax.all_to_all(activated.reshape(device_count, holding * cells, hidden),...  15.5 us
    pallas_call x4, Pallas kernels, gather(): pl.pallas_call(gather_kernel, in_specs=[pl.BlockSpec(memory_space=pltpu.S...  14.7 us
    pallas_call x1, Pallas kernels, serve(): pl.pallas_call(expert_kernel, grid=(steps,), in_specs=[pl.BlockSpec((coun...  13 us
    pallas_call x2, Pallas kernels, by_chunk(): pl.pallas_call(functools.partial(chunk_kernel, first), in_specs=[anywhere...  12.1 us
  transfers between devices with their start and end apart: 9, of which 6 were waited for; matrix products, arithmetic and copies ran while one was open for 5% of the time, Pallas kernels for 9%

profile of v2, /device:TPU:0, one launch (start us, length us, event | category | flops | bytes accessed | tf_op | source)
XLA Modules:
  0.0 454.4 jit_solution(16245128596385683139)
XLA Ops:
  7.8 0.6 broadcast_in_dim.66
  8.4 7.3 %all-to-all-start = ((bf16[32,1,128]{2,1,0:T(2,128)(2,1)}), bf16[32,1,128]{2,1,0:T(2,128)(2,1)S(1)}, u32[]{:S(2)}, u32[]{:S(2)}) async-start(bf16[32,1,128]{2,1,0:T(2,128)(2,1)} %broadcast_in_dim.66), calls=%async_computation | async-start | bytes 32768 | tf_op jit(solution)/shard_map/all_to_all | solution.py:248
  15.7 6.6 %shard_map.102 = bf16[16,2,128,1024]{3,2,1,0:T(8,128)(2,1)} custom-call(bf16[2,3584,1024]{2,1,0:T(8,128)(2,1)} %q_ref.1), custom_call_target="tpu_custom_call" | custom-call | bytes 16777216 | tf_op jit(solution)/shard_map/pallas_call | solution.py:142
  22.3 0.5 all-to-all-done
  22.8 4.9 %all-to-all-start.2 = ((bf16[16,2,128,1024]{3,2,1,0:T(8,128)(2,1)}), bf16[16,2,128,1024]{3,2,1,0:T(8,128)(2,1)}, u32[]{:S(2)}, u32[]{:S(2)}) async-start(bf16[16,2,128,1024]{3,2,1,0:T(8,128)(2,1)} %shard_map.102), calls=%async_computation.2 | async-start | bytes 16777216 | tf_op jit(solution)/shard_map/all_to_all | solution.py:275
  28.3 0.7 pad_maximum_fusion
  29.0 5.5 %shard_map.103 = bf16[16,2,96,1024]{3,2,1,0:T(8,128)(2,1)} custom-call(bf16[2,3584,1024]{2,1,0:T(8,128)(2,1)} %q_ref.1), custom_call_target="tpu_custom_call" | custom-call | bytes 12582912 | tf_op jit(solution)/shard_map/pallas_call | solution.py:142
  34.5 122.1 %all-gather.2.cloned.1.call-done = bf16[512,3712]{1,0:T(8,128)(2,1)} async-done(((bf16[16,3712]{1,0:T(8,128)(2,1)}), bf16[512,3712]{1,0:T(8,128)(2,1)}) %all-gather.2.cloned.1.call-update) | async-done | bytes 3801104 | tf_op jit(solution)/shard_map/all_gather | solution.py:272
  156.6 4.8 %all-to-all-start.1 = ((bf16[16,2,96,1024]{3,2,1,0:T(8,128)(2,1)}), bf16[16,2,96,1024]{3,2,1,0:T(8,128)(2,1)}, u32[]{:S(2)}, u32[]{:S(2)}) async-start(bf16[16,2,96,1024]{3,2,1,0:T(8,128)(2,1)} %shard_map.103), calls=%async_computation.1 | async-start | bytes 12582912 | tf_op jit(solution)/shard_map/all_to_all | solution.py:275
  162.0 0.8 reshape_reshape.3.s_ref
  162.9 0.2 convert_reduce_fusion.7
  163.1 0.6 add_select_fusion.6
  164.0 0.5 slice_clamp_fusion.15.index_ref
  165.2 0.2 compare_reduce_fusion.1
  165.6 0.7 convert_reduce_fusion.1
  166.4 3.1 shard_map.105
  169.5 1.4 collective-permute-start.16
  170.9 0.6 fusion.7
  171.5 0.6 select_reduce_fusion
  172.3 4.6 %convolution_convert_fusion.x_ref = bf16[256,3712]{1,0:T(8,128)(2,1)} fusion(bf16[512,3712]{1,0:T(8,128)(2,1)} %all-gather.2.cloned.1.call-done, s32[256]{0:T(256)S(1)} %select_n.446), kind=kOutput, calls=%fused_computation.32 | convolution fusion | flops 974159872 | bytes 5702656 | tf_op jit(solution)/shard_map/dot_general | solution.py:308
  176.9 13.0 %shard_map.104 = bf16[256,1024]{1,0:T(8,128)(2,1)} custom-call(bf16[256,3712]{1,0:T(8,128)(2,1)} %convolution_convert_fusion.x_ref, bf16[2,3584,1024]{2,1,0:T(8,128)(2,1)} %q_ref.1, f32[2,7,4,1024]{3,2,1,0:T(4,128)} %reshape_reshape.3.s_ref), custom_call_target="tpu_custom_call" | custom-call | flops 3758096384 | bytes 17039360 | tf_op jit(solution)/shard_map/pallas_call | solution.py:53
  189.8 91.4 %all-to-all-done.1 = bf16[16,2,96,1024]{3,2,1,0:T(8,128)(2,1)} async-done(((bf16[16,2,96,1024]{3,2,1,0:T(8,128)(2,1)}), bf16[16,2,96,1024]{3,2,1,0:T(8,128)(2,1)}, u32[]{:S(2)}, u32[]{:S(2)}) %all-to-all-start.1) | async-done | bytes 6291488 | tf_op jit(solution)/shard_map/all_to_all | solution.py:275
  281.3 2.6 all-to-all-start.3
  284.7 15.5 %all-to-all-done.3 = bf16[32,8,1024]{2,1,0:T(8,128)(2,1)S(1)} async-done(((bf16[32,8,1024]{2,1,0:T(8,128)(2,1)}), bf16[32,8,1024]{2,1,0:T(8,128)(2,1)S(1)}, u32[]{:S(2)}, u32[]{:S(2)}) %all-to-all-start.3) | async-done | bytes 524320 | tf_op jit(solution)/shard_map/all_to_all | solution.py:341
  300.2 0.8 copy-done.1
  301.0 4.4 conditional.2
  301.0 0.5 broadcast_clamp_fusion.index_ref
  301.5 3.9 branch_0_fun.2
  305.5 4.6 %all-to-all-start.5 = ((bf16[16,128,1024]{2,1,0:T(8,128)(2,1)}), bf16[16,128,1024]{2,1,0:T(8,128)(2,1)}, u32[]{:S(2)}, u32[]{:S(2)}) async-start(bf16[16,128,1024]{2,1,0:T(8,128)(2,1)} %get-tuple-element.300), calls=%async_computation.5 | async-start | bytes 8388608 | tf_op jit(solution)/shard_map/all_to_all | solution.py:351
  310.0 0.5 slice_clamp_fusion.14.index_ref
  310.5 3.0 shard_map.106
  313.7 80.1 %collective-permute-done.17 = bf16[8,96,1024]{2,1,0:T(8,128)(2,1)S(1)} collective-permute-done((bf16[8,96,1024]{2,1,0:T(8,128)(2,1)}, bf16[8,96,1024]{2,1,0:T(8,128)(2,1)S(1)}, u32[]{:S(2)}, u32[]{:S(2)}) %collective-permute-start.17) | collective-permute-done | bytes 1572896 | tf_op jit(solution)/shard_map/ppermute | solution.py:193
  393.8 5.3 %conditional.3 = (bf16[16,96,1024]{2,1,0:T(8,128)(2,1)}) conditional(s32[]{:T(128)} %clamp.38, (s32[16]{0:T(128)S(1)}, bf16[32,96,1024]{2,1,0:T(8,128)(2,1)}, bf16[8,96,1024]{2,1,0:T(8,128)(2,1)S(1)}) %tuple.75, (s32[16]{0:T(128)S(1)}, s32[16]{0:T(128)S(1)}, bf16[32,96,1024]{2,1,0:T(8,128)(2,1)}, ...), branch_computations={%region_18.19_spmd, %region_19.20_spmd, %region_20.21_spmd, %regio... | conditional | flops 24 | bytes 22020364 | solution.py:208
  393.8 0.5 broadcast_clamp_fusion.9.index_ref
  394.3 4.7 %branch_0_fun.3 = bf16[16,96,1024]{2,1,0:T(8,128)(2,1)} custom-call(s32[16]{0:T(128)} %broadcast_clamp_fusion.9.index_ref, bf16[32,96,1024]{2,1,0:T(8,128)(2,1)} %get-tuple-element.196.refs_0_, bf16[8,96,1024]{2,1,0:T(8,128)(2,1)S(1)} %get-tuple-element.197.refs_1_), custom_call_target="tpu_custom_call" | custom-call | bytes 6291456 | tf_op jit(solution)/shard_map/cond/branch_0_fun/pallas_call | solution.py:112
  399.1 3.8 all-to-all-start.4
  403.2 2.0 fusion.1
  405.2 0.9 slice.85
  406.3 0.7 copy.160
  407.6 0.8 compare_reduce_fusion
  408.5 0.7 fusion.3
  409.4 0.7 convert_reduce_fusion
  410.2 0.9 convert_reduce_fusion.4
  411.1 2.6 add_bitcast_fusion
  413.7 3.8 shard_map.107.refs_0_
  417.5 25.2 %all-to-all-done.4.blocks_ref = bf16[16,96,1024]{2,1,0:T(8,128)(2,1)S(1)} async-done(((bf16[16,96,1024]{2,1,0:T(8,128)(2,1)}), bf16[16,96,1024]{2,1,0:T(8,128)(2,1)S(1)}, u32[]{:S(2)}, u32[]{:S(2)}) %all-to-all-start.4) | async-done | bytes 3145760 | tf_op jit(solution)/shard_map/all_to_all | solution.py:357
  442.8 1.6 copy-done
  444.4 3.2 shard_map.108
  (84 shorter events, 4.3 us)
Async XLA Ops:
  8.4 14.3 %all-to-all-start = ((bf16[32,1,128]{2,1,0:T(2,128)(2,1)}), bf16[32,1,128]{2,1,0:T(2,128)(2,1)S(1)}, u32[]{:S(2)}, u32[]{:S(2)}) async-start(bf16[32,1,128]{2,1,0:T(2,128)(2,1)} %broadcast_in_dim.66), calls=%async_computation | async-start | bytes 32768 | tf_op jit(solution)/shard_map/all_to_all | solution.py:248
  22.8 5.0 %copy-start.18 = (s32[16,8]{0,1:T(8,128)S(1)}, s32[16,8]{0,1:T(8,128)}, u32[]{:S(2)}) copy-start(s32[16,8]{0,1:T(8,128)} %param.29) | copy-start | bytes 1540
  22.8 5.1 %copy-start.19 = (s32[16,8]{0,1:T(8,128)S(1)}, s32[16,8]{0,1:T(8,128)}, u32[]{:S(2)}) copy-start(s32[16,8]{0,1:T(8,128)} %param.30) | copy-start | bytes 1540
  22.8 5.2 %copy-start.17 = (bf16[2,28,8]{1,2,0:T(8,128)(2,1)S(1)}, bf16[2,28,8]{1,2,0:T(8,128)(2,1)}, u32[]{:S(2)}) copy-start(bf16[2,28,8]{1,2,0:T(8,128)(2,1)} %param.26) | copy-start | bytes 2692
  22.8 5.5 %copy-start.15 = (bf16[16,3584]{1,0:T(8,128)(2,1)S(1)}, bf16[16,3584]{1,0:T(8,128)(2,1)}, u32[]{:S(2)}) copy-start(bf16[16,3584]{1,0:T(8,128)(2,1)} %param.28) | copy-start | bytes 344068
  22.8 133.7 %all-to-all-start.2 = ((bf16[16,2,128,1024]{3,2,1,0:T(8,128)(2,1)}), bf16[16,2,128,1024]{3,2,1,0:T(8,128)(2,1)}, u32[]{:S(2)}, u32[]{:S(2)}) async-start(bf16[16,2,128,1024]{3,2,1,0:T(8,128)(2,1)} %shard_map.102), calls=%async_computation.2 | async-start | bytes 16777216 | tf_op jit(solution)/shard_map/all_to_all | solution.py:275
  27.7 128.8 %all-gather.2.cloned.1.call-start = ((), (), s32[]{:S(2)}) async-start(), calls=%async_computation.6 | async-start | bytes 3919872 | tf_op jit(solution)/shard_map/all_gather | solution.py:272
  156.5 8.0 %slice-start = ((bf16[512,3712]{1,0:T(8,128)(2,1)}), bf16[512,128]{1,0:T(8,128)(2,1)S(1)}, s32[]{:S(2)}) async-start(bf16[512,3712]{1,0:T(8,128)(2,1)} %all-gather.2.cloned.1.call-done), calls=%async_computation.7 | async-start | bytes 262144 | tf_op jit(solution)/shard_map/slice | solution.py:292
  156.6 124.7 %all-to-all-start.1 = ((bf16[16,2,96,1024]{3,2,1,0:T(8,128)(2,1)}), bf16[16,2,96,1024]{3,2,1,0:T(8,128)(2,1)}, u32[]{:S(2)}, u32[]{:S(2)}) async-start(bf16[16,2,96,1024]{3,2,1,0:T(8,128)(2,1)} %shard_map.103), calls=%async_computation.1 | async-start | bytes 12582912 | tf_op jit(solution)/shard_map/all_to_all | solution.py:275
  162.9 6.6 %copy-start.16 = (s32[32]{0:T(128)}, s32[32]{0:T(128)S(1)}, u32[]{:S(2)}) copy-start(s32[32]{0:T(128)S(1)} %convert_reduce_fusion.6) | copy-start | bytes 388
  169.5 115.2 %collective-permute-start.16 = (bf16[8,128,1024]{2,1,0:T(8,128)(2,1)}, bf16[8,128,1024]{2,1,0:T(8,128)(2,1)S(1)}, u32[]{:S(2)}, u32[]{:S(2)}) collective-permute-start(bf16[8,128,1024]{2,1,0:T(8,128)(2,1)} %shard_map.105), channel_id=1, source_target_pairs={{0,4},{1,5},{2,6},{3,7},{4,0},{5,1},{6,2},{7,3},{8,12},{9,13},{10,... | collective-permute-start | bytes 6291464 | tf_op jit(solution)/shard_map/ppermute | solution.py:193
  281.3 19.0 %all-to-all-start.3 = ((bf16[32,8,1024]{2,1,0:T(8,128)(2,1)}), bf16[32,8,1024]{2,1,0:T(8,128)(2,1)S(1)}, u32[]{:S(2)}, u32[]{:S(2)}) async-start(bf16[32,8,1024]{2,1,0:T(8,128)(2,1)} %bitcast.53), calls=%async_computation.3 | async-start | bytes 1048576 | tf_op jit(solution)/shard_map/all_to_all | solution.py:341
  300.2 0.8 copy-start.1
  305.5 93.6 %all-to-all-start.5 = ((bf16[16,128,1024]{2,1,0:T(8,128)(2,1)}), bf16[16,128,1024]{2,1,0:T(8,128)(2,1)}, u32[]{:S(2)}, u32[]{:S(2)}) async-start(bf16[16,128,1024]{2,1,0:T(8,128)(2,1)} %get-tuple-element.300), calls=%async_computation.5 | async-start | bytes 8388608 | tf_op jit(solution)/shard_map/all_to_all | solution.py:351
  313.6 80.2 %collective-permute-start.17 = (bf16[8,96,1024]{2,1,0:T(8,128)(2,1)}, bf16[8,96,1024]{2,1,0:T(8,128)(2,1)S(1)}, u32[]{:S(2)}, u32[]{:S(2)}) collective-permute-start(bf16[8,96,1024]{2,1,0:T(8,128)(2,1)} %shard_map.106), channel_id=1, source_target_pairs={{0,4},{1,5},{2,6},{3,7},{4,0},{5,1},{6,2},{7,3},{8,12},{9,13},{10,... | collective-permute-start | bytes 4718600 | tf_op jit(solution)/shard_map/ppermute | solution.py:193
  399.0 3.8 copy-start.20
  399.1 43.7 %all-to-all-start.4 = ((bf16[16,96,1024]{2,1,0:T(8,128)(2,1)}), bf16[16,96,1024]{2,1,0:T(8,128)(2,1)S(1)}, u32[]{:S(2)}, u32[]{:S(2)}) async-start(bf16[16,96,1024]{2,1,0:T(8,128)(2,1)} %get-tuple-element.301), calls=%async_computation.4 | async-start | bytes 6291456 | tf_op jit(solution)/shard_map/all_to_all | solution.py:357
  442.7 1.6 copy-start
Sparse Core Ops, SparseCore 0:
  32.0 124.4 all-gather.1
